TPU v7x, 128 devices: a whole 4x4x4 slice. The times are simulated.
128 devices in a mesh: space: 32 (over y, z_hi, x), head: 4 (over z_lo, core).
Axes of the slice: x: 4, y: 4, z: 4 (z_hi: 2, z_lo: 2; z = z_hi * 2 + z_lo), core: 2. Of those that a mesh axis runs over, the one named last changes fastest.
Arguments:
- levels: bfloat16 [13, 192, 48, 512], P(None, 'space'), may hold values from -6 to 6
- latent_query: bfloat16 [3, 512], replicated, may hold values from -200 to 200
- w_pq: bfloat16 [512, 512], P(None, 'head'), may hold values from -0.25 to 0.25
- w_pk: bfloat16 [512, 512], P(None, 'head'), may hold values from -0.25 to 0.25
- w_pv: bfloat16 [512, 512], P(None, 'head'), may hold values from -0.25 to 0.25
- w_po: bfloat16 [512, 512], P('head'), may hold values from -0.25 to 0.25
- layer_norm_gain: float32 [512], replicated, may hold values from 0.5 to 6
- window_query_weight: bfloat16 [512, 512], P(None, 'head'), may hold values from -0.25 to 0.25
- window_key_weight: bfloat16 [512, 512], P(None, 'head'), may hold values from -0.25 to 0.25
- window_value_weight: bfloat16 [512, 512], P(None, 'head'), may hold values from -0.25 to 0.25
- window_output_weight: bfloat16 [512, 512], P('head'), may hold values from -0.25 to 0.25
- cotangent: bfloat16 [3, 192, 48, 512], P(None, 'space'), may hold values from -6 to 6
Outputs:
- grad_levels: bfloat16 [13, 192, 48, 512], P(None, 'space', None, 'head')
All inputs are finite; a program needn't handle non-finite values.
Results may differ from a plain program's by a relative error of at most 0.034.
The roundings to bfloat16 on the way count: a program that leaves them out, or rounds other values in their place, can miss the bound.
Values may be sent and summed in bfloat16 or wider, within the bound.
A program may use at most 64 MiB of HBM per device.

v0:
```python
import functools

import jax
import jax.numpy as jnp
from jax import lax
from jax.experimental import pallas as pl
from jax.experimental.pallas import tpu as pltpu
from jax.sharding import PartitionSpec as P

X_CHIPS = 4
LEVELS = 13
CHUNKS = 7
WIDTH = 512
PATCH = 72
HALF = 108
SCALE = 32 ** (-0.5)
MESH = pl.DeviceIdType.MESH
BF = jnp.bfloat16
F32 = jnp.float32
PK, PV, PO, WO, WQ, WK, WV = range(7)
BY_COLUMN = (True, True, False, False, True, True, True)


def nn(left, right):
    return jnp.dot(left, right, preferred_element_type=F32)


def nt(left, right):
    return lax.dot_general(left, right, (((1,), (1,)), ((), ())), preferred_element_type=F32)


def rows(n):
    return lax.broadcasted_iota(jnp.int32, (n, 1), 0)


def cols(n):
    return lax.broadcasted_iota(jnp.int32, (1, n), 1)


def hot(condition):
    return jnp.where(condition, 1.0, 0.0).astype(BF)


def kernel(
    levels, lq_ref, wpq_ref, wpk, wpv, wpo, gain_ref, wq, wk, wv, wo, cot,
    out,
    lev, cotx, full, lqs, qbuf, qbt, ea, ead, sw, sp, pm, bias,
    xs, vs, ps, dps, cot_l, cot_win, lat_l, lat_in, ds_l, ds_in,
    win_q, win_k, win_v, win_o, g_q, g_k, g_v, zs, inv_s, ob, rv, fin,
    loc_sem, w_send, w_recv, q_send, q_recv, e_send, e_recv, a_send, a_recv, own_sem, out_sem,
):
    s = lax.axis_index("space")
    n = lax.axis_size("space")
    h = lax.axis_index("head")
    sib = h + 1 - 2 * lax.rem(h, 2)
    over = lax.rem(h + 2, 4)
    diag = 3 - h
    z_other = s + X_CHIPS - 2 * X_CHIPS * lax.rem(lax.div(s, X_CHIPS), 2)
    prev = lax.rem(s + n - 1, n)
    after = lax.rem(s + 1, n)
    weights = (wpk, wpv, wpo, wo, wq, wk, wv)

    def region(k, head, part):
        if BY_COLUMN[k]:
            along = slice(None) if part is None else pl.ds(256 * part, 256)
            return full.at[k, along, pl.ds(pl.multiple_of(head * 128, 128), 128)]
        if part is None:
            return full.at[k, pl.ds(pl.multiple_of(head * 128, 128), 128)]
        return full.at[k, pl.ds(pl.multiple_of(head * 128 + 64 * part, 64), 64)]

    def shard(k, part):
        if part is None:
            return weights[k]
        size = 256 if BY_COLUMN[k] else 64
        return weights[k].at[pl.ds(size * part, size)]

    def remote(src, dst, send, recv, device):
        return pltpu.make_async_remote_copy(
            src_ref=src, dst_ref=dst, send_sem=send, recv_sem=recv,
            device_id=device, device_id_type=MESH,
        )

    b0 = lax.div(12 * h + 6, 16)
    b1 = lax.rem(b0 + 1, 3)
    base = 12 * h + 6 - 16 * b0
    local = []
    for block, where in ((b0, 0), (b1, 16)):
        at = pl.ds(pl.multiple_of(16 * block, 16), 16)
        local.append((levels.at[:, :, at, :], lev.at[pl.ds(0, LEVELS), :, pl.ds(where, 16), :]))
        local.append((cot.at[:, :, at, :], cotx.at[:, :, pl.ds(where, 16), :]))
    for k in range(7):
        local.append((weights[k], region(k, h, None)))
    local = [
        pltpu.make_async_copy(src, dst, loc_sem.at[i]) for i, (src, dst) in enumerate(local)
    ]
    for copy in local:
        copy.start()

    barrier = pltpu.get_barrier_semaphore()
    for device in ((s, sib), (s, over), (s, diag), (z_other, over), (prev, h), (after, h)):
        pl.semaphore_signal(barrier, inc=1, device_id=device, device_id_type=MESH)
    pl.semaphore_wait(barrier, 6)

    sent = []

    def send(copy):
        copy.start()
        sent.append(copy)

    for k in range(7):
        send(remote(shard(k, 0), region(k, h, 0), w_send.at[k, 1], w_recv.at[k, 1], (s, over)))
        send(remote(shard(k, 1), region(k, h, 1), w_send.at[k, 2], w_recv.at[k, 2], (z_other, over)))
        send(remote(shard(k, None), region(k, h, None), w_send.at[k, 0], w_recv.at[k, 0], (s, sib)))

    lqs[...] = jnp.zeros_like(lqs)
    lqs[0:3, :] = lq_ref[...].astype(F32)
    lq16 = lqs[...].astype(BF)
    qbuf[h] = nn(lq16, wpq_ref[...]).astype(BF)
    for r, peer in enumerate((sib, over, diag)):
        send(remote(qbuf.at[h], qbuf.at[h], q_send.at[r], q_recv.at[r], (s, peer)))

    def wait_in(k, i, head, part, peer):
        remote(region(k, head, part), region(k, head, part), w_send.at[k, i], w_recv.at[k, i], (s, peer)).wait_recv()

    def relay(k):
        for part in range(2):
            wait_in(k, 1 + part, over, part, over)
            piece = region(k, over, part)
            send(remote(piece, piece, w_send.at[k, 3 + part], w_recv.at[k, 3 + part], (s, sib)))

    def have(k):
        local[4 + k].wait()
        wait_in(k, 0, sib, None, sib)
        for part in range(2):
            wait_in(k, 3 + part, diag, part, sib)

    lane_head = lax.div(cols(WIDTH), 32)
    for a in range(3):
        ea[a] = hot(rows(128) == a * 16 + lane_head)
        ead[a] = hot(lax.rem(rows(128), 64) == a * 16 + lane_head)
    w_row = lax.rem(rows(256), 128)
    w_a = lax.div(w_row, 36)
    w_k = lax.rem(w_row, 36)
    upper = rows(256) < 128
    w_patch = w_a * 72 + w_k + jnp.where(upper, 36, 0)
    w_col = jnp.where(w_row < HALF, w_patch, -1)
    sw[...] = hot(w_col == cols(224))
    p_a = lax.div(rows(224), 72)
    p_k = lax.rem(rows(224), 72)
    p_col = p_a * 36 + jnp.where(p_k >= 36, p_k - 36, 128 + p_k)
    sp[...] = hot(jnp.where(p_a < 3, p_col, -1) == cols(256))
    o_row = lax.div(rows(288), 48)
    o_lon = lax.rem(lax.rem(rows(288), 48) + 42, 48)
    o_col = lax.div(o_lon, 12) * 72 + o_row * 12 + lax.rem(o_lon, 12)
    pm[...] = hot(o_col == cols(288))
    pad_key = lax.rem(rows(256), 128) >= HALF
    crossing = jnp.logical_and((rows(256) < 128) != (cols(256) < 128), s == n - 1)
    bias[...] = jnp.where(jnp.logical_or(pad_key, crossing), -1e30, 0.0).astype(F32)
    lq_row = nn(hot(jnp.where(w_row < HALF, w_a, -1) == cols(16)), lq16)

    local[0].wait()
    local[2].wait()
    lev[LEVELS] = jnp.zeros((6, 32, WIDTH), BF)
    in_row = lax.div(rows(PATCH), 12)
    take = hot(in_row * 32 + base + lax.rem(rows(PATCH), 12) == cols(192))

    def pick(c, carry):
        two = [nn(take, lev[2 * c + i].reshape(192, WIDTH)) for i in range(2)]
        xs[c] = jnp.concatenate(two, axis=0).astype(BF)
        return carry

    lax.fori_loop(0, CHUNKS, pick, 0)

    local[1].wait()
    local[3].wait()
    h_row = rows(128)
    h_a = jnp.where(h_row < HALF, lax.div(h_row, 36), -1)
    h_k = lax.rem(h_row, 36)
    h_at = lax.div(h_k, 12) * 32 + base + lax.rem(h_k, 12)
    for half, keep in ((0, cot_l), (1, None)):
        total = None
        for a in range(3):
            spot = jnp.where(h_a == a, h_at + half * 96, -1)
            term = nn(hot(spot == cols(192)), cotx[a].reshape(192, WIDTH))
            total = term if total is None else total + term
        if half == 0:
            cot_l[...] = total.astype(BF)
            send(remote(cot_l, cot_win.at[pl.ds(128, 128)], e_send.at[0], e_recv.at[0], (prev, h)))
        else:
            cot_win[0:128] = total.astype(BF)

    for r, peer in enumerate((sib, over, diag)):
        remote(qbuf.at[peer], qbuf.at[peer], q_send.at[r], q_recv.at[r], (s, peer)).wait_recv()
    q16 = jnp.concatenate([qbuf[i] for i in range(4)], axis=1)
    q_rows = nn(hot(lax.div(lax.rem(rows(128), 64), 16) == cols(16)), q16)
    qbt[...] = jnp.where(lax.rem(rows(128), 16) == lane_head, q_rows, 0.0).astype(BF)
    relay(PK)
    relay(PV)
    have(PK)
    have(PV)

    def project(c, carry):
        x = xs[c]
        key = nn(x, full[PK]).astype(BF)
        ps[c] = nt(key, qbt[...]) * SCALE
        vs[c] = nn(x, full[PV]).astype(BF)
        return carry

    lax.fori_loop(0, CHUNKS, project, 0)
    relay(PO)

    def level(ref, l):
        return ref[l // 2, (l % 2) * PATCH:(l % 2 + 1) * PATCH]

    top = level(ps, 0)
    for l in range(1, LEVELS):
        top = jnp.maximum(top, level(ps, l))
    norm = jnp.zeros_like(top)
    for l in range(LEVELS):
        e = jnp.exp(level(ps, l) - top)
        ps[l // 2, (l % 2) * PATCH:(l % 2 + 1) * PATCH] = e
        norm = norm + e
    inverse = 1.0 / norm
    for l in range(LEVELS):
        ps[l // 2, (l % 2) * PATCH:(l % 2 + 1) * PATCH] = level(ps, l) * inverse
    ps[CHUNKS - 1, PATCH:] = jnp.zeros((PATCH, 128), F32)

    def mix(c, total):
        value = vs[c].astype(F32)
        prob = ps[c].astype(BF)
        new = []
        for a in range(3):
            both = nn(prob, ea[a]) * value
            new.append(total[a] + both[:PATCH] + both[PATCH:])
        return tuple(new)

    mixed = lax.fori_loop(0, CHUNKS, mix, tuple(jnp.zeros((PATCH, WIDTH), F32) for _ in range(3)))
    mixed = jnp.concatenate(list(mixed) + [jnp.zeros((8, WIDTH), F32)], axis=0).astype(BF)
    mixed = nn(sw[...], mixed).astype(BF)
    have(PO)
    latent = (lq_row + nn(mixed, full[PO])).astype(BF)
    lat_l[...] = latent[128:]
    send(remote(lat_l, lat_in, e_send.at[1], e_recv.at[1], (prev, h)))

    relay(WO)
    relay(WQ)
    have(WO)
    remote(cot_l, cot_win.at[pl.ds(128, 128)], e_send.at[0], e_recv.at[0], (prev, h)).wait_recv()
    win_o[...] = nt(cot_win[...], full[WO]).astype(BF)
    relay(WK)
    relay(WV)
    remote(lat_l, lat_in, e_send.at[1], e_recv.at[1], (prev, h)).wait_recv()
    z = jnp.concatenate([latent[:128], lat_in[...]], axis=0).astype(F32)
    z = z - jnp.mean(z, axis=-1, keepdims=True)
    inv = lax.rsqrt(jnp.mean(z * z, axis=-1, keepdims=True) + 1e-05)
    z = z * inv
    zs[...] = z
    inv_s[...] = jnp.broadcast_to(inv, (256, 128))
    normed = (z * gain_ref[...]).astype(BF)
    have(WQ)
    win_q[...] = nn(normed, full[WQ]).astype(BF)
    have(WK)
    win_k[...] = nn(normed, full[WK]).astype(BF)
    have(WV)
    win_v[...] = nn(normed, full[WV]).astype(BF)

    def attend(g, carry):
        lanes = pl.ds(pl.multiple_of(g * 128, 128), 128)
        qg, kg, vg, og = win_q[:, lanes], win_k[:, lanes], win_v[:, lanes], win_o[:, lanes]
        kt = kg.astype(F32).T.astype(BF)
        gk = jnp.zeros((256, 128), F32)
        gv = jnp.zeros((256, 128), F32)
        gq = []
        for i in range(4):
            mine = hot(lax.div(cols(128), 32) == i)
            qm = qg * mine
            om = og * mine
            score = nt(kg, qm) * SCALE + bias[...]
            e = jnp.exp(score - jnp.max(score, axis=0, keepdims=True))
            prob = e * (1.0 / jnp.sum(e, axis=0, keepdims=True))
            gv = gv + nn(prob.astype(BF), om)
            dp = nt(vg, om)
            dp = dp - jnp.sum(prob * dp, axis=0, keepdims=True)
            ds = (prob * dp * SCALE).astype(BF)
            gk = gk + nn(ds, qm)
            gq.append(nn(kt[32 * i:32 * i + 32], ds))
        g_k[:, lanes] = gk.astype(BF)
        g_v[:, lanes] = gv.astype(BF)
        g_q[:, lanes] = jnp.concatenate(gq, axis=0).T.astype(BF)
        return carry

    lax.fori_loop(0, 4, attend, 0)
    d = nt(g_q[...], full[WQ]) + nt(g_k[...], full[WK]) + nt(g_v[...], full[WV])
    d = d * gain_ref[...]
    z = zs[...]
    d = inv_s[:, 0:1] * (
        d - jnp.mean(d, axis=-1, keepdims=True) - z * jnp.mean(d * z, axis=-1, keepdims=True)
    )
    ds_l[...] = d[128:].astype(BF)
    send(remote(ds_l, ds_in, e_send.at[2], e_recv.at[2], (after, h)))
    grad_u = (cot_win[0:128].astype(F32) + d[:128]).astype(BF)
    remote(ds_l, ds_in, e_send.at[2], e_recv.at[2], (after, h)).wait_recv()
    grad_l = (cot_l[...].astype(F32) + ds_in[...].astype(F32)).astype(BF)
    grad = jnp.concatenate([grad_u, grad_l], axis=0)
    d_mixed = nt(grad, full[PO]).astype(BF)
    d_mixed = nn(sp[...], d_mixed)
    d_mixed = [d_mixed[PATCH * a:PATCH * (a + 1)] for a in range(3)]

    def level_dp(c, carry):
        value = vs[c].astype(F32)
        total = jnp.zeros((2 * PATCH, 128), F32)
        for a in range(3):
            prod = jnp.concatenate([d_mixed[a] * value[:PATCH], d_mixed[a] * value[PATCH:]], axis=0)
            high = prod.astype(BF)
            low = (prod - high.astype(F32)).astype(BF)
            total = total + nt(high, ead[a]) + nt(low, ead[a])
        dps[c] = total
        return carry

    lax.fori_loop(0, CHUNKS, level_dp, 0)
    mean = jnp.zeros((PATCH, 128), F32)
    for l in range(LEVELS):
        mean = mean + level(ps, l) * level(dps, l)
    low_lanes = cols(128) < 64

    def finish(c, carry):
        prob = ps[c]
        dp = dps[c]
        ds = prob * jnp.concatenate([dp[:PATCH] - mean, dp[PATCH:] - mean], axis=0) * SCALE
        high = ds.astype(BF).astype(F32)
        ds = jnp.where(low_lanes, high, ds - high).astype(BF)
        grad_key = nn(ds, qbt[...]).astype(BF)
        prob = prob.astype(BF)
        grad_value = jnp.zeros((2 * PATCH, WIDTH), F32)
        for a in range(3):
            wide = nn(prob, ea[a])
            grad_value = grad_value + jnp.concatenate(
                [d_mixed[a] * wide[:PATCH], d_mixed[a] * wide[PATCH:]], axis=0
            )
        ob[c] = (nt(grad_key, full[PK]) + nt(grad_value.astype(BF), full[PV])).astype(BF)
        return carry

    def own_part(c):
        lanes = pl.ds(pl.multiple_of(h * 128, 128), 128)
        return pltpu.make_async_copy(ob.at[c, :, lanes], rv.at[h, c], own_sem.at[c])

    for c in range(CHUNKS):
        finish(c, 0)
        size = pl.ds(0, 144 if c < CHUNKS - 1 else 80)
        for r, peer in enumerate((sib, over, diag)):
            lanes = pl.ds(pl.multiple_of(peer * 128, 128), 128)
            send(remote(
                ob.at[c, size, lanes], rv.at[h, c, size], a_send.at[c, r], a_recv.at[c, r], (s, peer)
            ))
        own_part(c).start()

    writes = []
    for c in range(CHUNKS):
        size = pl.ds(0, 144 if c < CHUNKS - 1 else 80)
        for r, peer in enumerate((sib, over, diag)):
            place = rv.at[peer, c, size]
            remote(place, place, a_send.at[c, r], a_recv.at[c, r], (s, peer)).wait_recv()
        own_part(c).wait()
        parts = []
        for j in range(4):
            if c < CHUNKS - 1:
                got = rv[j, c].astype(F32)
                parts.append(jnp.concatenate([got[:PATCH], got[PATCH:]], axis=1))
            else:
                parts.append(rv[j, c, 0:80].astype(F32)[:PATCH])
        got = nn(pm[...], jnp.concatenate(parts, axis=0).astype(BF)).astype(BF)
        for i in range(2 if c < CHUNKS - 1 else 1):
            fin[2 * c + i] = got[:, 128 * i:128 * (i + 1)]
        size = pl.ds(2 * c, 2 if c < CHUNKS - 1 else 1)
        copy = pltpu.make_async_copy(fin.at[size], out.at[size], out_sem.at[c])
        copy.start()
        writes.append(copy)
    for copy in writes:
        copy.wait()
    for copy in sent:
        copy.wait_send()


def per_device(levels, latent_query, w_pq, w_pk, w_pv, w_po, gain, wq, wk, wv, wo, cot):
    anywhere = pl.BlockSpec(memory_space=pl.ANY)
    vmem = pl.BlockSpec(memory_space=pltpu.VMEM)
    scratch = [
        pltpu.VMEM((14, 6, 32, WIDTH), BF),
        pltpu.VMEM((3, 6, 32, WIDTH), BF),
        pltpu.VMEM((7, WIDTH, WIDTH), BF),
        pltpu.VMEM((16, WIDTH), F32),
        pltpu.VMEM((4, 16, 128), BF),
        pltpu.VMEM((128, WIDTH), BF),
        pltpu.VMEM((3, 128, WIDTH), BF),
        pltpu.VMEM((3, 128, WIDTH), BF),
        pltpu.VMEM((256, 224), BF),
        pltpu.VMEM((224, 256), BF),
        pltpu.VMEM((288, 288), BF),
        pltpu.VMEM((256, 256), F32),
        pltpu.VMEM((CHUNKS, 144, WIDTH), BF),
        pltpu.VMEM((CHUNKS, 144, WIDTH), BF),
        pltpu.VMEM((CHUNKS, 144, 128), F32),
        pltpu.VMEM((CHUNKS, 144, 128), F32),
        pltpu.VMEM((128, WIDTH), BF),
        pltpu.VMEM((256, WIDTH), BF),
        pltpu.VMEM((128, WIDTH), BF),
        pltpu.VMEM((128, WIDTH), BF),
        pltpu.VMEM((128, WIDTH), BF),
        pltpu.VMEM((128, WIDTH), BF),
    ] + [pltpu.VMEM((256, WIDTH), BF) for _ in range(7)] + [
        pltpu.VMEM((256, WIDTH), F32),
        pltpu.VMEM((256, 128), F32),
        pltpu.VMEM((CHUNKS, 144, WIDTH), BF),
        pltpu.VMEM((4, CHUNKS, 144, 128), BF),
        pltpu.VMEM((14, 288, 128), BF),
    ] + [
        pltpu.SemaphoreType.DMA(shape)
        for shape in (
            (11,), (7, 5), (7, 5), (3,), (3,), (3,), (3,), (CHUNKS, 3), (CHUNKS, 3),
            (CHUNKS,), (CHUNKS,),
        )
    ]
    result = pl.pallas_call(
        kernel,
        out_shape=jax.ShapeDtypeStruct((LEVELS, 288, 128), BF),
        in_specs=[anywhere, vmem, vmem, anywhere, anywhere, anywhere, vmem,
                  anywhere, anywhere, anywhere, anywhere, anywhere],
        out_specs=anywhere,
        scratch_shapes=scratch,
        compiler_params=pltpu.CompilerParams(
            collective_id=0, has_side_effects=True, vmem_limit_bytes=48 * 1024 * 1024
        ),
        name="encoder_backward",
    )(levels, latent_query, w_pq, w_pk, w_pv, w_po, gain.reshape(1, WIDTH), wq, wk, wv, wo, cot)
    return result.reshape(LEVELS, 6, 48, 128)


def solution(mesh):
    placed = (
        P(None, "space", None, None),
        P(),
        P(None, "head"),
        P(None, "head"),
        P(None, "head"),
        P("head", None),
        P(),
        P(None, "head"),
        P(None, "head"),
        P(None, "head"),
        P("head", None),
        P(None, "space", None, None),
    )
    return jax.shard_map(
        per_device,
        mesh=mesh,
        in_specs=placed,
        out_specs=P(None, "space", None, "head"),
        check_vma=False,
    )
```

profile of v0, /device:TPU:1, one launch (start us, length us, event | category | flops | bytes accessed | tf_op | source)
XLA Modules:
  0.0 80.6 jit_solution(4784010034238398111)
XLA Ops:
  0.0 0.0 copy-start
  0.0 1.2 %copy-done = bf16[3,6,48,512]{3,2,1,0:T(8,128)(2,1)S(1)} copy-done((bf16[3,6,48,512]{3,2,1,0:T(8,128)(2,1)S(1)}, bf16[3,6,48,512]{3,2,1,0:T(8,128)(2,1)}, u32[]{:S(2)}) %copy-start) | copy-done | bytes 884760
  1.2 0.0 copy-start.1
  1.2 0.9 %copy-done.1 = bf16[512,128]{1,0:T(8,128)(2,1)S(1)} copy-done((bf16[512,128]{1,0:T(8,128)(2,1)S(1)}, bf16[512,128]{1,0:T(8,128)(2,1)}, u32[]{:S(2)}) %copy-start.1) | copy-done | bytes 131096
  2.1 0.0 copy-start.2
  2.1 0.9 %copy-done.2 = bf16[512,128]{1,0:T(8,128)(2,1)S(1)} copy-done((bf16[512,128]{1,0:T(8,128)(2,1)S(1)}, bf16[512,128]{1,0:T(8,128)(2,1)}, u32[]{:S(2)}) %copy-start.2) | copy-done | bytes 131096
  3.0 0.0 copy-start.3
  3.0 0.9 %copy-done.3 = bf16[512,128]{1,0:T(8,128)(2,1)S(1)} copy-done((bf16[512,128]{1,0:T(8,128)(2,1)S(1)}, bf16[512,128]{1,0:T(8,128)(2,1)}, u32[]{:S(2)}) %copy-start.3) | copy-done | bytes 131096
  3.9 0.0 copy-start.4
  3.9 0.9 %copy-done.4 = bf16[128,512]{1,0:T(8,128)(2,1)S(1)} copy-done((bf16[128,512]{1,0:T(8,128)(2,1)S(1)}, bf16[128,512]{1,0:T(8,128)(2,1)}, u32[]{:S(2)}) %copy-start.4) | copy-done | bytes 131096
  4.8 0.0 copy-start.5
  4.8 0.9 %copy-done.5 = bf16[512,128]{1,0:T(8,128)(2,1)S(1)} copy-done((bf16[512,128]{1,0:T(8,128)(2,1)S(1)}, bf16[512,128]{1,0:T(8,128)(2,1)}, u32[]{:S(2)}) %copy-start.5) | copy-done | bytes 131096
  5.7 0.0 copy-start.6
  5.7 0.9 %copy-done.6 = bf16[512,128]{1,0:T(8,128)(2,1)S(1)} copy-done((bf16[512,128]{1,0:T(8,128)(2,1)S(1)}, bf16[512,128]{1,0:T(8,128)(2,1)}, u32[]{:S(2)}) %copy-start.6) | copy-done | bytes 131096
  6.6 0.0 copy-start.7
  6.6 0.9 %copy-done.7 = bf16[512,128]{1,0:T(8,128)(2,1)S(1)} copy-done((bf16[512,128]{1,0:T(8,128)(2,1)S(1)}, bf16[512,128]{1,0:T(8,128)(2,1)}, u32[]{:S(2)}) %copy-start.7) | copy-done | bytes 131096
  7.5 0.0 copy-start.8
  7.5 0.9 %copy-done.8 = bf16[128,512]{1,0:T(8,128)(2,1)S(1)} copy-done((bf16[128,512]{1,0:T(8,128)(2,1)S(1)}, bf16[128,512]{1,0:T(8,128)(2,1)}, u32[]{:S(2)}) %copy-start.8) | copy-done | bytes 131096
  8.4 0.0 copy-start.9
  8.4 0.7 copy-done.9
  9.1 0.0 copy-start.10
  9.1 0.7 copy-done.10
  9.8 69.9 %encoder_backward.1 = bf16[13,288,128]{2,1,0:T(8,128)(2,1)S(1)} custom-call(bf16[13,6,48,512]{3,2,1,0:T(8,128)(2,1)} %levels.1, bf16[3,512]{1,0:T(4,128)(2,1)S(1)} %copy-done.9, bf16[512,128]{1,0:T(8,128)(2,1)S(1)} %copy-done.1, bf16[512,128]{1,0:T(8,128)(2,1)S(1)} %copy-done.2, bf16[512,128]{1,0:T(8,128)(2,1)S(1)} %copy-done.3, ...), custom_call_target="tpu_custom_call" | custom-call | tf_op jit(solution)/shard_map/encoder_backward/pallas_call | solution.py:423
  79.7 0.9 %copy.14 = bf16[13,6,48,128]{3,2,1,0:T(8,128)(2,1)} copy(bf16[13,6,48,128]{3,2,1,0:T(8,128)(2,1)S(1)} %bitcast.2) | data formatting | bytes 1916928
Async XLA Ops:
  0.0 1.2 %copy-start = (bf16[3,6,48,512]{3,2,1,0:T(8,128)(2,1)S(1)}, bf16[3,6,48,512]{3,2,1,0:T(8,128)(2,1)}, u32[]{:S(2)}) copy-start(bf16[3,6,48,512]{3,2,1,0:T(8,128)(2,1)} %cot.1) | copy-start | bytes 2654212
  1.2 0.9 %copy-start.1 = (bf16[512,128]{1,0:T(8,128)(2,1)S(1)}, bf16[512,128]{1,0:T(8,128)(2,1)}, u32[]{:S(2)}) copy-start(bf16[512,128]{1,0:T(8,128)(2,1)} %wpq_ref.1) | copy-start | bytes 393220
  2.1 0.9 %copy-start.2 = (bf16[512,128]{1,0:T(8,128)(2,1)S(1)}, bf16[512,128]{1,0:T(8,128)(2,1)}, u32[]{:S(2)}) copy-start(bf16[512,128]{1,0:T(8,128)(2,1)} %wpk.1) | copy-start | bytes 393220
  3.0 0.9 %copy-start.3 = (bf16[512,128]{1,0:T(8,128)(2,1)S(1)}, bf16[512,128]{1,0:T(8,128)(2,1)}, u32[]{:S(2)}) copy-start(bf16[512,128]{1,0:T(8,128)(2,1)} %wpv.1) | copy-start | bytes 393220
  3.9 0.9 %copy-start.4 = (bf16[128,512]{1,0:T(8,128)(2,1)S(1)}, bf16[128,512]{1,0:T(8,128)(2,1)}, u32[]{:S(2)}) copy-start(bf16[128,512]{1,0:T(8,128)(2,1)} %wpo.1) | copy-start | bytes 393220
  4.8 0.9 %copy-start.5 = (bf16[512,128]{1,0:T(8,128)(2,1)S(1)}, bf16[512,128]{1,0:T(8,128)(2,1)}, u32[]{:S(2)}) copy-start(bf16[512,128]{1,0:T(8,128)(2,1)} %wq.1) | copy-start | bytes 393220
  5.7 0.9 %copy-start.6 = (bf16[512,128]{1,0:T(8,128)(2,1)S(1)}, bf16[512,128]{1,0:T(8,128)(2,1)}, u32[]{:S(2)}) copy-start(bf16[512,128]{1,0:T(8,128)(2,1)} %wk.1) | copy-start | bytes 393220
  6.6 0.9 %copy-start.7 = (bf16[512,128]{1,0:T(8,128)(2,1)S(1)}, bf16[512,128]{1,0:T(8,128)(2,1)}, u32[]{:S(2)}) copy-start(bf16[512,128]{1,0:T(8,128)(2,1)} %wv.1) | copy-start | bytes 393220
  7.5 0.9 %copy-start.8 = (bf16[128,512]{1,0:T(8,128)(2,1)S(1)}, bf16[128,512]{1,0:T(8,128)(2,1)}, u32[]{:S(2)}) copy-start(bf16[128,512]{1,0:T(8,128)(2,1)} %wo.1) | copy-start | bytes 393220
  8.4 0.7 copy-start.9
  9.1 0.7 copy-start.10
where the time goes:
time: 81 us; the launch traced here: 80.6 us
  Pallas kernels  69.9 us (86%)
  local copies, waits for them, and re-layouts  10.7 us (13%)
    pallas_call x1, Pallas kernels, per_device(): pl.pallas_call(kernel, out_shape=jax.ShapeDtypeStruct((LEVELS, 288, 128),...  69.9 us
    unnamed x23, local copies, waits for them, and re-layouts  10.7 us

commit v1 on v0

v1 whole, which is shorter than its diff:
```python
import functools

import jax
import jax.numpy as jnp
from jax import lax
from jax.experimental import pallas as pl
from jax.experimental.pallas import tpu as pltpu
from jax.sharding import PartitionSpec as P

X_CHIPS = 4
LEVELS = 13
CHUNKS = 4
WIDTH = 512
PART = 40
START = (0, 160, 320, 480)
SIZE = (160, 160, 160, 48)
DEPTH = (4, 4, 4, 1)
SENT = (144, 144, 144, 48)
VMEM_LIMIT = 62 * 1024 * 1024
SCALE = 32 ** (-0.5)
MESH = pl.DeviceIdType.MESH
BF = jnp.bfloat16
F32 = jnp.float32
PK, PV, PO, WO, WQ, WK, WV = range(7)
BY_COLUMN = (True, True, False, False, True, True, True)


def nn(left, right):
    return jnp.dot(left, right, preferred_element_type=F32)


def nt(left, right):
    return lax.dot_general(left, right, (((1,), (1,)), ((), ())), preferred_element_type=F32)


def rows(n):
    return lax.broadcasted_iota(jnp.int32, (n, 1), 0)


def cols(n):
    return lax.broadcasted_iota(jnp.int32, (1, n), 1)


def hot(condition):
    return jnp.where(condition, 1.0, 0.0).astype(BF)


def kernel(
    levels, lq_in, wpq_in, wpk, wpv, wpo, gain_in, wq, wk, wv, wo, cot,
    out,
    lq_ref, wpq_ref, gain_ref, lev, cotx, full, lqs, qbuf, qbt, ea, ead, pack, unpack, pack1, unpack1, bias,
    xs, vs, ps, dps, cot_l, cot_win, lat_l, lat_in, ds_l, ds_in,
    win_q, win_k, win_v, win_o, g_q, g_k, g_v, zs, inv_s, ob, rv, fin,
    loc_sem, w_send, w_recv, q_send, q_recv, e_send, e_recv, a_send, a_recv, own_sem, out_sem,
):
    s = lax.axis_index("space")
    n = lax.axis_size("space")
    h = lax.axis_index("head")
    sib = h + 1 - 2 * lax.rem(h, 2)
    over = lax.rem(h + 2, 4)
    diag = 3 - h
    z_other = s + X_CHIPS - 2 * X_CHIPS * lax.rem(lax.div(s, X_CHIPS), 2)
    prev = lax.rem(s + n - 1, n)
    after = lax.rem(s + 1, n)
    weights = (wpk, wpv, wpo, wo, wq, wk, wv)

    def region(k, head, part):
        if BY_COLUMN[k]:
            along = slice(None) if part is None else pl.ds(256 * part, 256)
            return full.at[k, along, pl.ds(pl.multiple_of(head * 128, 128), 128)]
        if part is None:
            return full.at[k, pl.ds(pl.multiple_of(head * 128, 128), 128)]
        return full.at[k, pl.ds(pl.multiple_of(head * 128 + 64 * part, 64), 64)]

    def shard(k, part):
        if part is None:
            return weights[k]
        size = 256 if BY_COLUMN[k] else 64
        return weights[k].at[pl.ds(size * part, size)]

    def remote(src, dst, send, recv, device):
        return pltpu.make_async_remote_copy(
            src_ref=src, dst_ref=dst, send_sem=send, recv_sem=recv,
            device_id=device, device_id_type=MESH,
        )

    b0 = lax.div(12 * h + 6, 16)
    b1 = lax.rem(b0 + 1, 3)
    base = 12 * h + 6 - 16 * b0
    local = []
    for block, where in ((b0, 0), (b1, 16)):
        at = pl.ds(pl.multiple_of(16 * block, 16), 16)
        local.append((levels.at[:, :, at, :], lev.at[pl.ds(0, LEVELS), :, pl.ds(where, 16), :]))
        local.append((cot.at[:, :, at, :], cotx.at[:, :, pl.ds(where, 16), :]))
    for k in range(7):
        local.append((weights[k], region(k, h, None)))
    for src, dst in ((lq_in, lq_ref), (wpq_in, wpq_ref), (gain_in, gain_ref)):
        local.append((src, dst))
    local = [
        pltpu.make_async_copy(src, dst, loc_sem.at[i]) for i, (src, dst) in enumerate(local)
    ]
    for copy in local:
        copy.start()

    barrier = pltpu.get_barrier_semaphore()
    for device in ((s, sib), (s, over), (s, diag), (z_other, over), (prev, h), (after, h)):
        pl.semaphore_signal(barrier, inc=1, device_id=device, device_id_type=MESH)
    pl.semaphore_wait(barrier, 6)

    sent = []

    def send(copy):
        copy.start()
        sent.append(copy)

    for k in range(7):
        send(remote(shard(k, 0), region(k, h, 0), w_send.at[k, 1], w_recv.at[k, 1], (s, over)))
        send(remote(shard(k, 1), region(k, h, 1), w_send.at[k, 2], w_recv.at[k, 2], (z_other, over)))
        send(remote(shard(k, None), region(k, h, None), w_send.at[k, 0], w_recv.at[k, 0], (s, sib)))

    local[11].wait()
    local[12].wait()
    local[13].wait()
    lqs[...] = jnp.zeros_like(lqs)
    lqs[0:3, :] = lq_ref[...].astype(F32)
    lq16 = lqs[...].astype(BF)
    qbuf[h] = nn(lq16, wpq_ref[...]).astype(BF)
    for r, peer in enumerate((sib, over, diag)):
        send(remote(qbuf.at[h], qbuf.at[h], q_send.at[r], q_recv.at[r], (s, peer)))

    def wait_in(k, i, head, part, peer):
        remote(region(k, head, part), region(k, head, part), w_send.at[k, i], w_recv.at[k, i], (s, peer)).wait_recv()

    def relay(k):
        for part in range(2):
            wait_in(k, 1 + part, over, part, over)
            piece = region(k, over, part)
            send(remote(piece, piece, w_send.at[k, 3 + part], w_recv.at[k, 3 + part], (s, sib)))

    def have(k):
        local[4 + k].wait()
        wait_in(k, 0, sib, None, sib)
        for part in range(2):
            wait_in(k, 3 + part, diag, part, sib)

    lane_head = lax.div(cols(WIDTH), 32)
    for a in range(3):
        ea[a] = hot(rows(128) == a * 16 + lane_head)
        ead[a] = hot(lax.rem(rows(128), 64) == a * 16 + lane_head)
    k_row = lax.div(rows(144), 36) * PART + lax.rem(rows(144), 36)
    pack[...] = hot(k_row == cols(160))
    pack1[...] = hot(jnp.where(rows(48) < 36, rows(48), -1) == cols(PART))
    o_row = lax.rem(rows(288), 144)
    o_lon = lax.rem(lax.rem(o_row, 48) + 42, 48)
    o_cell = lax.div(o_row, 48) * 12 + lax.rem(o_lon, 12)
    unpack[...] = hot(lax.div(o_lon, 12) * 72 + lax.div(rows(288), 144) * 36 + o_cell == cols(288))
    unpack1[...] = hot((lax.div(o_lon, 12) * PART + o_cell)[:144] == cols(160))
    in_half = lax.rem(rows(256), 128)
    pad_key = jnp.logical_or(in_half >= 120, lax.rem(in_half, PART) >= 36)
    crossing = jnp.logical_and((rows(256) < 128) != (cols(256) < 128), s == n - 1)
    bias[...] = jnp.where(jnp.logical_or(pad_key, crossing), -1e30, 0.0).astype(F32)
    lq_row = nn(hot(lax.div(rows(128), PART) == cols(16)), lq16)

    local[0].wait()
    local[2].wait()
    cell = lax.rem(rows(80), PART)
    spot = lax.div(rows(80), PART) * 96 + lax.div(cell, 12) * 32 + base + lax.rem(cell, 12)
    take = hot(jnp.where(cell < 36, spot, -1) == cols(192))
    for c in range(CHUNKS):
        got = [nn(take, lev[4 * c + i].reshape(192, WIDTH)) for i in range(DEPTH[c])]
        for half in range(2):
            part = [one[PART * half:PART * (half + 1)] for one in got]
            if DEPTH[c] == 1:
                part.append(jnp.zeros((8, WIDTH), F32))
            xs[half, START[c]:START[c] + SIZE[c]] = jnp.concatenate(part, axis=0).astype(BF)

    local[1].wait()
    local[3].wait()
    cell = lax.rem(rows(128), PART)
    spot = lax.div(cell, 12) * 32 + base + lax.rem(cell, 12)
    spot = jnp.where(cell < 36, spot, -1000)
    for half in range(2):
        total = None
        for a in range(3):
            here = jnp.where(lax.div(rows(128), PART) == a, spot + half * 96, -1)
            term = nn(hot(here == cols(192)), cotx[a].reshape(192, WIDTH))
            total = term if total is None else total + term
        if half == 0:
            cot_l[...] = total.astype(BF)
            send(remote(cot_l, cot_win.at[pl.ds(128, 128)], e_send.at[0], e_recv.at[0], (prev, h)))
        else:
            cot_win[0:128] = total.astype(BF)

    for r, peer in enumerate((sib, over, diag)):
        remote(qbuf.at[peer], qbuf.at[peer], q_send.at[r], q_recv.at[r], (s, peer)).wait_recv()
    q16 = jnp.concatenate([qbuf[i] for i in range(4)], axis=1)
    q_rows = nn(hot(lax.div(lax.rem(rows(128), 64), 16) == cols(16)), q16)
    qbt[...] = jnp.where(lax.rem(rows(128), 16) == lane_head, q_rows, 0.0).astype(BF)
    relay(PK)
    relay(PV)
    have(PK)
    have(PV)

    def level(ref, half, l):
        return ref[half, PART * l:PART * (l + 1)]

    def spread(value, depth):
        return value[:PART * depth].reshape(depth, PART, value.shape[-1])

    def forward(half):
        for c in range(CHUNKS):
            at = slice(START[c], START[c] + SIZE[c])
            x = xs[half, at]
            key = nn(x, full[PK]).astype(BF)
            ps[half, at] = nt(key, qbt[...]) * SCALE
            vs[half, at] = nn(x, full[PV]).astype(BF)
        top = level(ps, half, 0)
        for l in range(1, LEVELS):
            top = jnp.maximum(top, level(ps, half, l))
        norm = jnp.zeros_like(top)
        for l in range(LEVELS):
            e = jnp.exp(level(ps, half, l) - top)
            ps[half, PART * l:PART * (l + 1)] = e
            norm = norm + e
        inverse = 1.0 / norm
        for l in range(LEVELS):
            ps[half, PART * l:PART * (l + 1)] = level(ps, half, l) * inverse
        ps[half, PART * LEVELS:] = jnp.zeros((8, 128), F32)

    def mix(half):
        total = [jnp.zeros((PART, WIDTH), F32) for _ in range(3)]
        for c in range(CHUNKS):
            at = slice(START[c], START[c] + SIZE[c])
            value = vs[half, at].astype(F32)
            prob = ps[half, at].astype(BF)
            for a in range(3):
                total[a] = total[a] + jnp.sum(spread(nn(prob, ea[a]) * value, DEPTH[c]), axis=0)
        mixed = jnp.concatenate(total + [jnp.zeros((8, WIDTH), F32)], axis=0).astype(BF)
        return (lq_row + nn(mixed, full[PO])).astype(BF)

    forward(0)
    relay(PO)
    have(PO)
    lat_l[...] = mix(0)
    send(remote(lat_l, lat_in, e_send.at[1], e_recv.at[1], (prev, h)))
    relay(WO)
    forward(1)
    relay(WQ)
    latent = mix(1)

    have(WO)
    remote(cot_l, cot_win.at[pl.ds(128, 128)], e_send.at[0], e_recv.at[0], (prev, h)).wait_recv()
    win_o[...] = nt(cot_win[...], full[WO]).astype(BF)
    relay(WK)
    relay(WV)
    remote(lat_l, lat_in, e_send.at[1], e_recv.at[1], (prev, h)).wait_recv()
    z = jnp.concatenate([latent, lat_in[...]], axis=0).astype(F32)
    z = z - jnp.mean(z, axis=-1, keepdims=True)
    inv = lax.rsqrt(jnp.mean(z * z, axis=-1, keepdims=True) + 1e-05)
    z = z * inv
    zs[...] = z
    inv_s[...] = jnp.broadcast_to(inv, (256, 128))
    normed = (z * gain_ref[...]).astype(BF)
    have(WQ)
    win_q[...] = nn(normed, full[WQ]).astype(BF)
    have(WK)
    win_k[...] = nn(normed, full[WK]).astype(BF)
    have(WV)
    win_v[...] = nn(normed, full[WV]).astype(BF)

    def attend(g, carry):
        lanes = pl.ds(pl.multiple_of(g * 128, 128), 128)
        qg, kg, vg, og = win_q[:, lanes], win_k[:, lanes], win_v[:, lanes], win_o[:, lanes]
        kt = kg.astype(F32).T.astype(BF)
        gk = jnp.zeros((256, 128), F32)
        gv = jnp.zeros((256, 128), F32)
        gq = []
        for i in range(4):
            mine = hot(lax.div(cols(128), 32) == i)
            qm = qg * mine
            om = og * mine
            score = nt(kg, qm) * SCALE + bias[...]
            e = jnp.exp(score - jnp.max(score, axis=0, keepdims=True))
            prob = e * (1.0 / jnp.sum(e, axis=0, keepdims=True))
            gv = gv + nn(prob.astype(BF), om)
            dp = nt(vg, om)
            dp = dp - jnp.sum(prob * dp, axis=0, keepdims=True)
            ds = (prob * dp * SCALE).astype(BF)
            gk = gk + nn(ds, qm)
            gq.append(nn(kt[32 * i:32 * i + 32], ds))
        g_k[:, lanes] = gk.astype(BF)
        g_v[:, lanes] = gv.astype(BF)
        g_q[:, lanes] = jnp.concatenate(gq, axis=0).T.astype(BF)
        return carry

    lax.fori_loop(0, 4, attend, 0)

    def shift_grad(at):
        d = nt(g_q[at], full[WQ]) + nt(g_k[at], full[WK]) + nt(g_v[at], full[WV])
        d = d * gain_ref[...]
        z = zs[at]
        return inv_s[at, 0:1] * (
            d - jnp.mean(d, axis=-1, keepdims=True) - z * jnp.mean(d * z, axis=-1, keepdims=True)
        )

    ds_l[...] = shift_grad(slice(128, 256)).astype(BF)
    send(remote(ds_l, ds_in, e_send.at[2], e_recv.at[2], (after, h)))

    low_lanes = cols(128) < 64

    def own_part(half, c):
        lanes = pl.ds(pl.multiple_of(h * 128, 128), 128)
        at = pl.ds(144 * c, SENT[c])
        return pltpu.make_async_copy(ob.at[half, at, lanes], rv.at[h, half, at], own_sem.at[half, c])

    def backward(half, grad):
        d_mixed = nt(grad, full[PO]).astype(BF).astype(F32)
        d_mixed = [d_mixed[PART * a:PART * (a + 1)] for a in range(3)]
        for c in range(CHUNKS):
            size = PART * DEPTH[c]
            value = spread(vs[half, START[c]:START[c] + SIZE[c]].astype(F32), DEPTH[c])
            total = jnp.zeros((size, 128), F32)
            for a in range(3):
                prod = (value * d_mixed[a][None]).reshape(size, WIDTH)
                high = prod.astype(BF)
                low = (prod - high.astype(F32)).astype(BF)
                total = total + nt(high, ead[a]) + nt(low, ead[a])
            dps[START[c]:START[c] + size] = total
        mean = jnp.zeros((PART, 128), F32)
        for l in range(LEVELS):
            mean = mean + level(ps, half, l) * dps[PART * l:PART * (l + 1)]
        for c in range(CHUNKS):
            size = PART * DEPTH[c]
            prob = ps[half, START[c]:START[c] + size]
            dp = spread(dps[START[c]:START[c] + size], DEPTH[c])
            ds = prob * (dp - mean[None]).reshape(size, 128) * SCALE
            high = ds.astype(BF).astype(F32)
            ds = jnp.where(low_lanes, high, ds - high).astype(BF)
            grad_key = nn(ds, qbt[...]).astype(BF)
            prob = prob.astype(BF)
            grad_value = jnp.zeros((DEPTH[c], PART, WIDTH), F32)
            for a in range(3):
                grad_value = grad_value + d_mixed[a][None] * spread(nn(prob, ea[a]), DEPTH[c])
            grad_value = grad_value.reshape(size, WIDTH).astype(BF)
            total = (nt(grad_key, full[PK]) + nt(grad_value, full[PV])).astype(BF)
            total = nn(pack[...] if DEPTH[c] == 4 else pack1[...], total).astype(BF)
            ob[half, 144 * c:144 * c + SENT[c]] = total
            at = pl.ds(144 * c, SENT[c])
            for r, peer in ((1, over), (2, diag), (0, sib)):
                lanes = pl.ds(pl.multiple_of(peer * 128, 128), 128)
                send(remote(
                    ob.at[half, at, lanes], rv.at[h, half, at],
                    a_send.at[half, c, r], a_recv.at[half, c, r], (s, peer),
                ))
            own_part(half, c).start()

    grad = cot_win[0:128].astype(F32) + shift_grad(slice(0, 128))
    backward(1, grad.astype(BF))
    remote(ds_l, ds_in, e_send.at[2], e_recv.at[2], (after, h)).wait_recv()
    grad = cot_l[...].astype(F32) + ds_in[...].astype(F32)
    backward(0, grad.astype(BF))

    writes = []
    for half in (1, 0):
        for c in range(CHUNKS):
            at = pl.ds(144 * c, SENT[c])
            for r, peer in enumerate((sib, over, diag)):
                place = rv.at[peer, half, at]
                remote(place, place, a_send.at[half, c, r], a_recv.at[half, c, r], (s, peer)).wait_recv()
            own_part(half, c).wait()
            parts = []
            for j in range(4):
                got = rv[j, half, 144 * c:144 * c + SENT[c]].astype(F32)
                parts.append(jnp.concatenate([got[:72], got[72:]], axis=1) if DEPTH[c] == 4 else got[:PART])
            got = jnp.concatenate(parts, axis=0).astype(BF)
            got = nn(unpack[...] if DEPTH[c] == 4 else unpack1[...], got).astype(BF)
            for i in range(DEPTH[c]):
                up, along = 144 * (i % 2), 128 * (i // 2)
                fin[4 * c + i, 144 * half:144 * (half + 1)] = got[up:up + 144, along:along + 128]
            at = (pl.ds(4 * c, DEPTH[c]), pl.ds(144 * half, 144))
            copy = pltpu.make_async_copy(fin.at[at], out.at[at], out_sem.at[half, c])
            copy.start()
            writes.append(copy)
    for copy in writes:
        copy.wait()
    for copy in sent:
        copy.wait_send()


def per_device(levels, latent_query, w_pq, w_pk, w_pv, w_po, gain, wq, wk, wv, wo, cot):
    anywhere = pl.BlockSpec(memory_space=pl.ANY)
    scratch = [
        pltpu.VMEM((3, WIDTH), BF),
        pltpu.VMEM((WIDTH, 128), BF),
        pltpu.VMEM((1, WIDTH), F32),
        pltpu.VMEM((LEVELS, 6, 32, WIDTH), BF),
        pltpu.VMEM((3, 6, 32, WIDTH), BF),
        pltpu.VMEM((7, WIDTH, WIDTH), BF),
        pltpu.VMEM((16, WIDTH), F32),
        pltpu.VMEM((4, 16, 128), BF),
        pltpu.VMEM((128, WIDTH), BF),
        pltpu.VMEM((3, 128, WIDTH), BF),
        pltpu.VMEM((3, 128, WIDTH), BF),
        pltpu.VMEM((144, 160), BF),
        pltpu.VMEM((288, 288), BF),
        pltpu.VMEM((48, PART), BF),
        pltpu.VMEM((144, 160), BF),
        pltpu.VMEM((256, 256), F32),
        pltpu.VMEM((2, 528, WIDTH), BF),
        pltpu.VMEM((2, 528, WIDTH), BF),
        pltpu.VMEM((2, 528, 128), F32),
        pltpu.VMEM((528, 128), F32),
        pltpu.VMEM((128, WIDTH), BF),
        pltpu.VMEM((256, WIDTH), BF),
        pltpu.VMEM((128, WIDTH), BF),
        pltpu.VMEM((128, WIDTH), BF),
        pltpu.VMEM((128, WIDTH), BF),
        pltpu.VMEM((128, WIDTH), BF),
    ] + [pltpu.VMEM((256, WIDTH), BF) for _ in range(7)] + [
        pltpu.VMEM((256, WIDTH), F32),
        pltpu.VMEM((256, 128), F32),
        pltpu.VMEM((2, 480, WIDTH), BF),
        pltpu.VMEM((4, 2, 480, 128), BF),
        pltpu.VMEM((LEVELS, 288, 128), BF),
    ] + [
        pltpu.SemaphoreType.DMA(shape)
        for shape in (
            (14,), (7, 5), (7, 5), (3,), (3,), (3,), (3,), (2, CHUNKS, 3), (2, CHUNKS, 3),
            (2, CHUNKS), (2, CHUNKS),
        )
    ]
    result = pl.pallas_call(
        kernel,
        out_shape=jax.ShapeDtypeStruct((LEVELS, 288, 128), BF),
        in_specs=[anywhere] * 12,
        out_specs=anywhere,
        scratch_shapes=scratch,
        compiler_params=pltpu.CompilerParams(
            collective_id=0, has_side_effects=True, vmem_limit_bytes=VMEM_LIMIT
        ),
        name="encoder_backward",
    )(levels, latent_query, w_pq, w_pk, w_pv, w_po, gain.reshape(1, WIDTH), wq, wk, wv, wo, cot)
    return result.reshape(LEVELS, 6, 48, 128)


def solution(mesh):
    placed = (
        P(None, "space", None, None),
        P(),
        P(None, "head"),
        P(None, "head"),
        P(None, "head"),
        P("head", None),
        P(),
        P(None, "head"),
        P(None, "head"),
        P(None, "head"),
        P("head", None),
        P(None, "space", None, None),
    )
    return jax.shard_map(
        per_device,
        mesh=mesh,
        in_specs=placed,
        out_specs=P(None, "space", None, "head"),
        check_vma=False,
    )
```

time: 81 us -> 62.6 us (0.77)
  Pallas kernels: 69.9 us -> 60.2 us
  local copies, waits for them, and re-layouts: 10.7 us -> 2.19 us
    pallas_call x1, Pallas kernels: 69.9 us -> 60.2 us  [per_device(): pl.pallas_call(kernel, out_shape=jax.ShapeDtypeStruct((LEVELS, 288, 128),...]
    unnamed x23 -> x1, local copies, waits for them, and re-layouts: 10.7 us -> 2.19 us
where the time goes in v1:
time: 62.6 us; the launch traced here: 62.4 us
  Pallas kernels  60.2 us (96%)
  local copies, waits for them, and re-layouts  2.19 us (3%)
    pallas_call x1, Pallas kernels, per_device(): pl.pallas_call(kernel, out_shape=jax.ShapeDtypeStruct((LEVELS, 288, 128),...  60.2 us
    unnamed x1, local copies, waits for them, and re-layouts  2.19 us

profile of v1, /device:TPU:1, one launch (start us, length us, event | category | flops | bytes accessed | tf_op | source)
XLA Modules:
  0.0 62.4 jit_solution(17382596906606122833)
XLA Ops:
  0.0 60.2 %encoder_backward.1 = bf16[13,288,128]{2,1,0:T(8,128)(2,1)} custom-call(bf16[13,6,48,512]{3,2,1,0:T(8,128)(2,1)} %levels.1, bf16[3,512]{1,0:T(4,128)(2,1)} %lq_in.1, bf16[512,128]{1,0:T(8,128)(2,1)} %wpq_in.1, bf16[512,128]{1,0:T(8,128)(2,1)} %wpk.1, bf16[512,128]{1,0:T(8,128)(2,1)} %wpv.1, bf16[128,512]{1,0:T(8,128)(2,1)} %wpo.1, f32[1,512]{1,0:T(1,128)} %bitcast.3, ...), custom_call_target="tpu_custom_call" | custom-call | tf_op jit(solution)/shard_map/encoder_backward/pallas_call | solution.py:432
  60.2 2.2 %copy.14 = bf16[13,6,48,128]{3,2,1,0:T(8,128)(2,1)} copy(bf16[13,6,48,128]{3,2,1,0:T(8,128)(2,1)} %bitcast.2) | data formatting | bytes 1916928

commit v2 on v1

--- a/solution.py
+++ b/solution.py
@@ -64,7 +64,7 @@
     after = lax.rem(s + 1, n)
     weights = (wpk, wpv, wpo, wo, wq, wk, wv)
 
-    def region(k, head, part):
+    def region(k, head, part=None):
         if BY_COLUMN[k]:
             along = slice(None) if part is None else pl.ds(256 * part, 256)
             return full.at[k, along, pl.ds(pl.multiple_of(head * 128, 128), 128)]
@@ -73,8 +73,6 @@
         return full.at[k, pl.ds(pl.multiple_of(head * 128 + 64 * part, 64), 64)]
 
     def shard(k, part):
-        if part is None:
-            return weights[k]
         size = 256 if BY_COLUMN[k] else 64
         return weights[k].at[pl.ds(size * part, size)]
 
@@ -93,7 +91,7 @@
         local.append((levels.at[:, :, at, :], lev.at[pl.ds(0, LEVELS), :, pl.ds(where, 16), :]))
         local.append((cot.at[:, :, at, :], cotx.at[:, :, pl.ds(where, 16), :]))
     for k in range(7):
-        local.append((weights[k], region(k, h, None)))
+        local.append((weights[k], region(k, h)))
     for src, dst in ((lq_in, lq_ref), (wpq_in, wpq_ref), (gain_in, gain_ref)):
         local.append((src, dst))
     local = [
@@ -103,7 +101,9 @@
         copy.start()
 
     barrier = pltpu.get_barrier_semaphore()
-    for device in ((s, sib), (s, over), (s, diag), (z_other, over), (prev, h), (after, h)):
+    for device in (
+        (s, sib), (s, over), (s, diag), (z_other, over), (prev, h), (after, h),
+    ):
         pl.semaphore_signal(barrier, inc=1, device_id=device, device_id_type=MESH)
     pl.semaphore_wait(barrier, 6)
 
@@ -116,7 +116,7 @@
     for k in range(7):
         send(remote(shard(k, 0), region(k, h, 0), w_send.at[k, 1], w_recv.at[k, 1], (s, over)))
         send(remote(shard(k, 1), region(k, h, 1), w_send.at[k, 2], w_recv.at[k, 2], (z_other, over)))
-        send(remote(shard(k, None), region(k, h, None), w_send.at[k, 0], w_recv.at[k, 0], (s, sib)))
+        send(remote(weights[k], region(k, h), w_send.at[k, 0], w_recv.at[k, 0], (s, sib)))
 
     local[11].wait()
     local[12].wait()
@@ -128,20 +128,20 @@
     for r, peer in enumerate((sib, over, diag)):
         send(remote(qbuf.at[h], qbuf.at[h], q_send.at[r], q_recv.at[r], (s, peer)))
 
-    def wait_in(k, i, head, part, peer):
-        remote(region(k, head, part), region(k, head, part), w_send.at[k, i], w_recv.at[k, i], (s, peer)).wait_recv()
+    def wait_in(k, i, piece, device):
+        remote(piece, piece, w_send.at[k, i], w_recv.at[k, i], device).wait_recv()
 
     def relay(k):
-        for part in range(2):
-            wait_in(k, 1 + part, over, part, over)
+        for part, device in enumerate(((s, over), (z_other, over))):
             piece = region(k, over, part)
+            wait_in(k, 1 + part, piece, device)
             send(remote(piece, piece, w_send.at[k, 3 + part], w_recv.at[k, 3 + part], (s, sib)))
 
     def have(k):
         local[4 + k].wait()
-        wait_in(k, 0, sib, None, sib)
+        wait_in(k, 0, region(k, sib), (s, sib))
         for part in range(2):
-            wait_in(k, 3 + part, diag, part, sib)
+            wait_in(k, 3 + part, region(k, diag, part), (s, sib))
 
     lane_head = lax.div(cols(WIDTH), 32)
     for a in range(3):
@@ -157,7 +157,7 @@
     unpack1[...] = hot((lax.div(o_lon, 12) * PART + o_cell)[:144] == cols(160))
     in_half = lax.rem(rows(256), 128)
     pad_key = jnp.logical_or(in_half >= 120, lax.rem(in_half, PART) >= 36)
-    crossing = jnp.logical_and((rows(256) < 128) != (cols(256) < 128), s == n - 1)
+    crossing = jnp.logical_and((rows(256) < 128) != (cols(256) < 128), s == 0)
     bias[...] = jnp.where(jnp.logical_or(pad_key, crossing), -1e30, 0.0).astype(F32)
     lq_row = nn(hot(lax.div(rows(128), PART) == cols(16)), lq16)
 
@@ -179,15 +179,15 @@
     cell = lax.rem(rows(128), PART)
     spot = lax.div(cell, 12) * 32 + base + lax.rem(cell, 12)
     spot = jnp.where(cell < 36, spot, -1000)
-    for half in range(2):
+    for half in (1, 0):
         total = None
         for a in range(3):
             here = jnp.where(lax.div(rows(128), PART) == a, spot + half * 96, -1)
             term = nn(hot(here == cols(192)), cotx[a].reshape(192, WIDTH))
             total = term if total is None else total + term
-        if half == 0:
+        if half == 1:
             cot_l[...] = total.astype(BF)
-            send(remote(cot_l, cot_win.at[pl.ds(128, 128)], e_send.at[0], e_recv.at[0], (prev, h)))
+            send(remote(cot_l, cot_win.at[pl.ds(128, 128)], e_send.at[0], e_recv.at[0], (after, h)))
         else:
             cot_win[0:128] = total.astype(BF)
 
@@ -238,22 +238,22 @@
         mixed = jnp.concatenate(total + [jnp.zeros((8, WIDTH), F32)], axis=0).astype(BF)
         return (lq_row + nn(mixed, full[PO])).astype(BF)
 
-    forward(0)
     relay(PO)
+    forward(1)
+    relay(WO)
+    relay(WQ)
     have(PO)
-    lat_l[...] = mix(0)
-    send(remote(lat_l, lat_in, e_send.at[1], e_recv.at[1], (prev, h)))
-    relay(WO)
-    forward(1)
-    relay(WQ)
-    latent = mix(1)
-
-    have(WO)
-    remote(cot_l, cot_win.at[pl.ds(128, 128)], e_send.at[0], e_recv.at[0], (prev, h)).wait_recv()
-    win_o[...] = nt(cot_win[...], full[WO]).astype(BF)
+    lat_l[...] = mix(1)
+    send(remote(lat_l, lat_in, e_send.at[1], e_recv.at[1], (after, h)))
     relay(WK)
     relay(WV)
-    remote(lat_l, lat_in, e_send.at[1], e_recv.at[1], (prev, h)).wait_recv()
+    forward(0)
+    latent = mix(0)
+
+    have(WO)
+    remote(cot_l, cot_win.at[pl.ds(128, 128)], e_send.at[0], e_recv.at[0], (after, h)).wait_recv()
+    win_o[...] = nt(cot_win[...], full[WO]).astype(BF)
+    remote(lat_l, lat_in, e_send.at[1], e_recv.at[1], (after, h)).wait_recv()
     z = jnp.concatenate([latent, lat_in[...]], axis=0).astype(F32)
     z = z - jnp.mean(z, axis=-1, keepdims=True)
     inv = lax.rsqrt(jnp.mean(z * z, axis=-1, keepdims=True) + 1e-05)
@@ -268,32 +268,35 @@
     have(WV)
     win_v[...] = nn(normed, full[WV]).astype(BF)
 
-    def attend(g, carry):
-        lanes = pl.ds(pl.multiple_of(g * 128, 128), 128)
-        qg, kg, vg, og = win_q[:, lanes], win_k[:, lanes], win_v[:, lanes], win_o[:, lanes]
-        kt = kg.astype(F32).T.astype(BF)
-        gk = jnp.zeros((256, 128), F32)
-        gv = jnp.zeros((256, 128), F32)
-        gq = []
-        for i in range(4):
-            mine = hot(lax.div(cols(128), 32) == i)
-            qm = qg * mine
-            om = og * mine
-            score = nt(kg, qm) * SCALE + bias[...]
-            e = jnp.exp(score - jnp.max(score, axis=0, keepdims=True))
-            prob = e * (1.0 / jnp.sum(e, axis=0, keepdims=True))
-            gv = gv + nn(prob.astype(BF), om)
-            dp = nt(vg, om)
-            dp = dp - jnp.sum(prob * dp, axis=0, keepdims=True)
-            ds = (prob * dp * SCALE).astype(BF)
-            gk = gk + nn(ds, qm)
-            gq.append(nn(kt[32 * i:32 * i + 32], ds))
-        g_k[:, lanes] = gk.astype(BF)
-        g_v[:, lanes] = gv.astype(BF)
-        g_q[:, lanes] = jnp.concatenate(gq, axis=0).T.astype(BF)
-        return carry
-
-    lax.fori_loop(0, 4, attend, 0)
+    def head_scores(i):
+        lanes = slice(128 * (i // 4), 128 * (i // 4) + 128)
+        mine = hot(lax.div(cols(128), 32) == i % 4)
+        qm, om = win_q[:, lanes] * mine, win_o[:, lanes] * mine
+        return qm, om, nt(win_k[:, lanes], qm), nt(win_v[:, lanes], om)
+
+    following = head_scores(0)
+    for i in range(16):
+        qm, om, score, dp = following
+        if i < 15:
+            following = head_scores(i + 1)
+        if i % 4 == 0:
+            lanes = slice(32 * i, 32 * i + 128)
+            kt = win_k[:, lanes].astype(F32).T.astype(BF)
+            gk = jnp.zeros((256, 128), F32)
+            gv = jnp.zeros((256, 128), F32)
+            gq = []
+        score = score * SCALE + bias[...]
+        e = jnp.exp(score - jnp.max(score, axis=0, keepdims=True))
+        prob = e * (1.0 / jnp.sum(e, axis=0, keepdims=True))
+        dp = dp - jnp.sum(prob * dp, axis=0, keepdims=True)
+        ds = (prob * dp * SCALE).astype(BF)
+        gv = gv + nn(prob.astype(BF), om)
+        gk = gk + nn(ds, qm)
+        gq.append(nn(kt[32 * (i % 4):32 * (i % 4) + 32], ds))
+        if i % 4 == 3:
+            g_k[:, lanes] = gk.astype(BF)
+            g_v[:, lanes] = gv.astype(BF)
+            g_q[:, lanes] = jnp.concatenate(gq, axis=0).T.astype(BF)
 
     def shift_grad(at):
         d = nt(g_q[at], full[WQ]) + nt(g_k[at], full[WK]) + nt(g_v[at], full[WV])
@@ -304,7 +307,7 @@
         )
 
     ds_l[...] = shift_grad(slice(128, 256)).astype(BF)
-    send(remote(ds_l, ds_in, e_send.at[2], e_recv.at[2], (after, h)))
+    send(remote(ds_l, ds_in, e_send.at[2], e_recv.at[2], (prev, h)))
 
     low_lanes = cols(128) < 64
 
@@ -355,13 +358,13 @@
             own_part(half, c).start()
 
     grad = cot_win[0:128].astype(F32) + shift_grad(slice(0, 128))
+    backward(0, grad.astype(BF))
+    remote(ds_l, ds_in, e_send.at[2], e_recv.at[2], (prev, h)).wait_recv()
+    grad = cot_l[...].astype(F32) + ds_in[...].astype(F32)
     backward(1, grad.astype(BF))
-    remote(ds_l, ds_in, e_send.at[2], e_recv.at[2], (after, h)).wait_recv()
-    grad = cot_l[...].astype(F32) + ds_in[...].astype(F32)
-    backward(0, grad.astype(BF))
 
     writes = []
-    for half in (1, 0):
+    for half in (0, 1):
         for c in range(CHUNKS):
             at = pl.ds(144 * c, SENT[c])
             for r, peer in enumerate((sib, over, diag)):

time: 62.6 us -> 55.7 us (0.89)
  Pallas kernels: 60.2 us -> 53.4 us
    pallas_call x1, Pallas kernels: 60.2 us -> 53.4 us  [per_device(): pl.pallas_call(kernel, out_shape=jax.ShapeDtypeStruct((LEVELS, 288, 128),...]
where the time goes in v2:
time: 55.7 us; the launch traced here: 55.6 us
  Pallas kernels  53.4 us (96%)
  local copies, waits for them, and re-layouts  2.19 us (4%)
    pallas_call x1, Pallas kernels, per_device(): pl.pallas_call(kernel, out_shape=jax.ShapeDtypeStruct((LEVELS, 288, 128),...  53.4 us
    unnamed x1, local copies, waits for them, and re-layouts  2.19 us

profile of v2, /device:TPU:1, one launch (start us, length us, event | category | flops | bytes accessed | tf_op | source)
XLA Modules:
  0.0 55.6 jit_solution(8790029760334220762)
XLA Ops:
  0.0 53.4 %encoder_backward.1 = bf16[13,288,128]{2,1,0:T(8,128)(2,1)} custom-call(bf16[13,6,48,512]{3,2,1,0:T(8,128)(2,1)} %levels.1, bf16[3,512]{1,0:T(4,128)(2,1)} %lq_in.1, bf16[512,128]{1,0:T(8,128)(2,1)} %wpq_in.1, bf16[512,128]{1,0:T(8,128)(2,1)} %wpk.1, bf16[512,128]{1,0:T(8,128)(2,1)} %wpv.1, bf16[128,512]{1,0:T(8,128)(2,1)} %wpo.1, f32[1,512]{1,0:T(1,128)} %bitcast.3, ...), custom_call_target="tpu_custom_call" | custom-call | tf_op jit(solution)/shard_map/encoder_backward/pallas_call | solution.py:435
  53.4 2.2 %copy.14 = bf16[13,6,48,128]{3,2,1,0:T(8,128)(2,1)} copy(bf16[13,6,48,128]{3,2,1,0:T(8,128)(2,1)} %bitcast.2) | data formatting | bytes 1916928

commit v3 on v2

--- a/solution.py
+++ b/solution.py
@@ -16,7 +16,7 @@
 SIZE = (160, 160, 160, 48)
 DEPTH = (4, 4, 4, 1)
 SENT = (144, 144, 144, 48)
-VMEM_LIMIT = 62 * 1024 * 1024
+VMEM_LIMIT = 60 * 1024 * 1024
 SCALE = 32 ** (-0.5)
 MESH = pl.DeviceIdType.MESH
 BF = jnp.bfloat16
@@ -50,8 +50,8 @@
     out,
     lq_ref, wpq_ref, gain_ref, lev, cotx, full, lqs, qbuf, qbt, ea, ead, pack, unpack, pack1, unpack1, bias,
     xs, vs, ps, dps, cot_l, cot_win, lat_l, lat_in, ds_l, ds_in,
-    win_q, win_k, win_v, win_o, g_q, g_k, g_v, zs, inv_s, ob, rv, fin,
-    loc_sem, w_send, w_recv, q_send, q_recv, e_send, e_recv, a_send, a_recv, own_sem, out_sem,
+    win_q, win_k, win_v, win_o, g_q, g_k, g_v, zs, inv_s, ob, rv,
+    loc_sem, w_send, w_recv, q_send, q_recv, e_send, e_recv, a_send, a_recv, own_sem,
 ):
     s = lax.axis_index("space")
     n = lax.axis_size("space")
@@ -113,10 +113,13 @@
         copy.start()
         sent.append(copy)
 
-    for k in range(7):
+    def scatter(k):
         send(remote(shard(k, 0), region(k, h, 0), w_send.at[k, 1], w_recv.at[k, 1], (s, over)))
         send(remote(shard(k, 1), region(k, h, 1), w_send.at[k, 2], w_recv.at[k, 2], (z_other, over)))
         send(remote(weights[k], region(k, h), w_send.at[k, 0], w_recv.at[k, 0], (s, sib)))
+
+    for k in (PK, PV):
+        scatter(k)
 
     local[11].wait()
     local[12].wait()
@@ -127,6 +130,8 @@
     qbuf[h] = nn(lq16, wpq_ref[...]).astype(BF)
     for r, peer in enumerate((sib, over, diag)):
         send(remote(qbuf.at[h], qbuf.at[h], q_send.at[r], q_recv.at[r], (s, peer)))
+    for k in (PO, WO, WQ, WK, WV):
+        scatter(k)
 
     def wait_in(k, i, piece, device):
         remote(piece, piece, w_send.at[k, i], w_recv.at[k, i], device).wait_recv()
@@ -363,7 +368,6 @@
     grad = cot_l[...].astype(F32) + ds_in[...].astype(F32)
     backward(1, grad.astype(BF))
 
-    writes = []
     for half in (0, 1):
         for c in range(CHUNKS):
             at = pl.ds(144 * c, SENT[c])
@@ -379,13 +383,7 @@
             got = nn(unpack[...] if DEPTH[c] == 4 else unpack1[...], got).astype(BF)
             for i in range(DEPTH[c]):
                 up, along = 144 * (i % 2), 128 * (i // 2)
-                fin[4 * c + i, 144 * half:144 * (half + 1)] = got[up:up + 144, along:along + 128]
-            at = (pl.ds(4 * c, DEPTH[c]), pl.ds(144 * half, 144))
-            copy = pltpu.make_async_copy(fin.at[at], out.at[at], out_sem.at[half, c])
-            copy.start()
-            writes.append(copy)
-    for copy in writes:
-        copy.wait()
+                out[4 * c + i, 144 * half:144 * (half + 1)] = got[up:up + 144, along:along + 128]
     for copy in sent:
         copy.wait_send()
 
@@ -424,19 +422,18 @@
         pltpu.VMEM((256, 128), F32),
         pltpu.VMEM((2, 480, WIDTH), BF),
         pltpu.VMEM((4, 2, 480, 128), BF),
-        pltpu.VMEM((LEVELS, 288, 128), BF),
     ] + [
         pltpu.SemaphoreType.DMA(shape)
         for shape in (
             (14,), (7, 5), (7, 5), (3,), (3,), (3,), (3,), (2, CHUNKS, 3), (2, CHUNKS, 3),
-            (2, CHUNKS), (2, CHUNKS),
+            (2, CHUNKS),
         )
     ]
     result = pl.pallas_call(
         kernel,
-        out_shape=jax.ShapeDtypeStruct((LEVELS, 288, 128), BF),
+        out_shape=pltpu.VMEM((LEVELS, 288, 128), BF),
         in_specs=[anywhere] * 12,
-        out_specs=anywhere,
+        out_specs=pl.BlockSpec(memory_space=pltpu.VMEM),
         scratch_shapes=scratch,
         compiler_params=pltpu.CompilerParams(
             collective_id=0, has_side_effects=True, vmem_limit_bytes=VMEM_LIMIT

time: 55.7 us -> 51.7 us (0.928)
  Pallas kernels: 53.4 us -> 50.6 us
  local copies, waits for them, and re-layouts: 2.19 us -> 0.94 us
    pallas_call x1, Pallas kernels: 53.4 us -> 50.6 us  [per_device(): pl.pallas_call(kernel, out_shape=pltpu.VMEM((LEVELS, 288, 128), BF), in_s...]
    unnamed x1, local copies, waits for them, and re-layouts: 2.19 us -> 0.94 us
where the time goes in v3:
time: 51.7 us; the launch traced here: 51.6 us
  Pallas kernels  50.6 us (98%)
  local copies, waits for them, and re-layouts  0.94 us (2%)
    pallas_call x1, Pallas kernels, per_device(): pl.pallas_call(kernel, out_shape=pltpu.VMEM((LEVELS, 288, 128), BF), in_s...  50.6 us

profile of v3, /device:TPU:1, one launch (start us, length us, event | category | flops | bytes accessed | tf_op | source)
XLA Modules:
  0.0 51.6 jit_solution(6688985719408158725)
XLA Ops:
  0.0 50.6 %encoder_backward.1 = bf16[13,288,128]{2,1,0:T(8,128)(2,1)S(1)} custom-call(bf16[13,6,48,512]{3,2,1,0:T(8,128)(2,1)} %levels.1, bf16[3,512]{1,0:T(4,128)(2,1)} %lq_in.1, bf16[512,128]{1,0:T(8,128)(2,1)} %wpq_in.1, bf16[512,128]{1,0:T(8,128)(2,1)} %wpk.1, bf16[512,128]{1,0:T(8,128)(2,1)} %wpv.1, bf16[128,512]{1,0:T(8,128)(2,1)} %wpo.1, f32[1,512]{1,0:T(1,128)} %bitcast.3, ...), custom_call_target="tpu_custom_call" | custom-call | tf_op jit(solution)/shard_map/encoder_backward/pallas_call | solution.py:432
  50.7 0.9 %copy.14 = bf16[13,6,48,128]{3,2,1,0:T(8,128)(2,1)} copy(bf16[13,6,48,128]{3,2,1,0:T(8,128)(2,1)S(1)} %bitcast.2) | data formatting | bytes 1916928

commit v4 on v3

--- a/solution.py
+++ b/solution.py
@@ -18,6 +18,7 @@
 SENT = (144, 144, 144, 48)
 VMEM_LIMIT = 60 * 1024 * 1024
 SCALE = 32 ** (-0.5)
+LOG2E = 1.4426950408889634
 MESH = pl.DeviceIdType.MESH
 BF = jnp.bfloat16
 F32 = jnp.float32
@@ -82,6 +83,12 @@
             device_id=device, device_id_type=MESH,
         )
 
+    barrier = pltpu.get_barrier_semaphore()
+    for device in (
+        (s, sib), (s, over), (s, diag), (z_other, over), (prev, h), (after, h),
+    ):
+        pl.semaphore_signal(barrier, inc=1, device_id=device, device_id_type=MESH)
+
     b0 = lax.div(12 * h + 6, 16)
     b1 = lax.rem(b0 + 1, 3)
     base = 12 * h + 6 - 16 * b0
@@ -97,29 +104,8 @@
     local = [
         pltpu.make_async_copy(src, dst, loc_sem.at[i]) for i, (src, dst) in enumerate(local)
     ]
-    for copy in local:
+    for copy in local[11:] + local[:11]:
         copy.start()
-
-    barrier = pltpu.get_barrier_semaphore()
-    for device in (
-        (s, sib), (s, over), (s, diag), (z_other, over), (prev, h), (after, h),
-    ):
-        pl.semaphore_signal(barrier, inc=1, device_id=device, device_id_type=MESH)
-    pl.semaphore_wait(barrier, 6)
-
-    sent = []
-
-    def send(copy):
-        copy.start()
-        sent.append(copy)
-
-    def scatter(k):
-        send(remote(shard(k, 0), region(k, h, 0), w_send.at[k, 1], w_recv.at[k, 1], (s, over)))
-        send(remote(shard(k, 1), region(k, h, 1), w_send.at[k, 2], w_recv.at[k, 2], (z_other, over)))
-        send(remote(weights[k], region(k, h), w_send.at[k, 0], w_recv.at[k, 0], (s, sib)))
-
-    for k in (PK, PV):
-        scatter(k)
 
     local[11].wait()
     local[12].wait()
@@ -128,9 +114,23 @@
     lqs[0:3, :] = lq_ref[...].astype(F32)
     lq16 = lqs[...].astype(BF)
     qbuf[h] = nn(lq16, wpq_ref[...]).astype(BF)
+
+    pl.semaphore_wait(barrier, 6)
+
+    sent = []
+
+    def send(copy):
+        copy.start()
+        sent.append(copy)
+
+    def scatter(k):
+        send(remote(shard(k, 0), region(k, h, 0), w_send.at[k, 1], w_recv.at[k, 1], (s, over)))
+        send(remote(shard(k, 1), region(k, h, 1), w_send.at[k, 2], w_recv.at[k, 2], (z_other, over)))
+        send(remote(weights[k], region(k, h), w_send.at[k, 0], w_recv.at[k, 0], (s, sib)))
+
     for r, peer in enumerate((sib, over, diag)):
         send(remote(qbuf.at[h], qbuf.at[h], q_send.at[r], q_recv.at[r], (s, peer)))
-    for k in (PO, WO, WQ, WK, WV):
+    for k in range(7):
         scatter(k)
 
     def wait_in(k, i, piece, device):
@@ -201,24 +201,17 @@
     q16 = jnp.concatenate([qbuf[i] for i in range(4)], axis=1)
     q_rows = nn(hot(lax.div(lax.rem(rows(128), 64), 16) == cols(16)), q16)
     qbt[...] = jnp.where(lax.rem(rows(128), 16) == lane_head, q_rows, 0.0).astype(BF)
-    relay(PK)
-    relay(PV)
-    have(PK)
-    have(PV)
-
     def level(ref, half, l):
         return ref[half, PART * l:PART * (l + 1)]
 
     def spread(value, depth):
         return value[:PART * depth].reshape(depth, PART, value.shape[-1])
 
-    def forward(half):
+    def score_levels(half):
         for c in range(CHUNKS):
             at = slice(START[c], START[c] + SIZE[c])
-            x = xs[half, at]
-            key = nn(x, full[PK]).astype(BF)
+            key = nn(xs[half, at], full[PK]).astype(BF)
             ps[half, at] = nt(key, qbt[...]) * SCALE
-            vs[half, at] = nn(x, full[PV]).astype(BF)
         top = level(ps, half, 0)
         for l in range(1, LEVELS):
             top = jnp.maximum(top, level(ps, half, l))
@@ -232,6 +225,11 @@
             ps[half, PART * l:PART * (l + 1)] = level(ps, half, l) * inverse
         ps[half, PART * LEVELS:] = jnp.zeros((8, 128), F32)
 
+    def project_values(half):
+        for c in range(CHUNKS):
+            at = slice(START[c], START[c] + SIZE[c])
+            vs[half, at] = nn(xs[half, at], full[PV]).astype(BF)
+
     def mix(half):
         total = [jnp.zeros((PART, WIDTH), F32) for _ in range(3)]
         for c in range(CHUNKS):
@@ -240,38 +238,55 @@
             prob = ps[half, at].astype(BF)
             for a in range(3):
                 total[a] = total[a] + jnp.sum(spread(nn(prob, ea[a]) * value, DEPTH[c]), axis=0)
-        mixed = jnp.concatenate(total + [jnp.zeros((8, WIDTH), F32)], axis=0).astype(BF)
+        return jnp.concatenate(total + [jnp.zeros((8, WIDTH), F32)], axis=0).astype(BF)
+
+    def latent_of(mixed):
         return (lq_row + nn(mixed, full[PO])).astype(BF)
 
+    relay(PK)
+    have(PK)
+    score_levels(1)
+    relay(PV)
+    score_levels(0)
+    have(PV)
+    project_values(1)
+    mixed = mix(1)
     relay(PO)
-    forward(1)
+    have(PO)
+    lat_l[...] = latent_of(mixed)
+    send(remote(lat_l, lat_in, e_send.at[1], e_recv.at[1], (after, h)))
     relay(WO)
+    project_values(0)
+    latent = latent_of(mix(0))
+
+    def normalise(at, value):
+        z = value.astype(F32)
+        z = z - jnp.mean(z, axis=-1, keepdims=True)
+        inv = lax.rsqrt(jnp.mean(z * z, axis=-1, keepdims=True) + 1e-05)
+        z = z * inv
+        zs[at] = z
+        inv_s[at] = jnp.broadcast_to(inv, (128, 128))
+        return (z * gain_ref[...]).astype(BF)
+
+    kept, lent = slice(0, 128), slice(128, 256)
+    normed = normalise(kept, latent)
     relay(WQ)
-    have(PO)
-    lat_l[...] = mix(1)
-    send(remote(lat_l, lat_in, e_send.at[1], e_recv.at[1], (after, h)))
-    relay(WK)
-    relay(WV)
-    forward(0)
-    latent = mix(0)
-
     have(WO)
     remote(cot_l, cot_win.at[pl.ds(128, 128)], e_send.at[0], e_recv.at[0], (after, h)).wait_recv()
     win_o[...] = nt(cot_win[...], full[WO]).astype(BF)
+    relay(WK)
+    have(WQ)
+    win_q[kept] = nn(normed, full[WQ]).astype(BF)
+    relay(WV)
+    have(WK)
+    win_k[kept] = nn(normed, full[WK]).astype(BF)
     remote(lat_l, lat_in, e_send.at[1], e_recv.at[1], (after, h)).wait_recv()
-    z = jnp.concatenate([latent, lat_in[...]], axis=0).astype(F32)
-    z = z - jnp.mean(z, axis=-1, keepdims=True)
-    inv = lax.rsqrt(jnp.mean(z * z, axis=-1, keepdims=True) + 1e-05)
-    z = z * inv
-    zs[...] = z
-    inv_s[...] = jnp.broadcast_to(inv, (256, 128))
-    normed = (z * gain_ref[...]).astype(BF)
-    have(WQ)
-    win_q[...] = nn(normed, full[WQ]).astype(BF)
-    have(WK)
-    win_k[...] = nn(normed, full[WK]).astype(BF)
+    borrowed = normalise(lent, lat_in[...])
+    win_q[lent] = nn(borrowed, full[WQ]).astype(BF)
+    win_k[lent] = nn(borrowed, full[WK]).astype(BF)
     have(WV)
-    win_v[...] = nn(normed, full[WV]).astype(BF)
+    win_v[kept] = nn(normed, full[WV]).astype(BF)
+    win_v[lent] = nn(borrowed, full[WV]).astype(BF)
 
     def head_scores(i):
         lanes = slice(128 * (i // 4), 128 * (i // 4) + 128)
@@ -279,29 +294,37 @@
         qm, om = win_q[:, lanes] * mine, win_o[:, lanes] * mine
         return qm, om, nt(win_k[:, lanes], qm), nt(win_v[:, lanes], om)
 
+    state = {}
+
+    def head_grads(i, prob, ds, qm, om):
+        lanes = slice(128 * (i // 4), 128 * (i // 4) + 128)
+        if i % 4 == 0:
+            state["kt"] = win_k[:, lanes].astype(F32).T.astype(BF)
+            state["gk"] = jnp.zeros((256, 128), F32)
+            state["gv"] = jnp.zeros((256, 128), F32)
+            state["gq"] = []
+        state["gv"] = state["gv"] + nn(prob, om)
+        state["gk"] = state["gk"] + nn(ds, qm)
+        state["gq"].append(nn(state["kt"][32 * (i % 4):32 * (i % 4) + 32], ds))
+        if i % 4 == 3:
+            g_k[:, lanes] = state["gk"].astype(BF)
+            g_v[:, lanes] = state["gv"].astype(BF)
+            g_q[:, lanes] = jnp.concatenate(state["gq"], axis=0).T.astype(BF)
+
     following = head_scores(0)
+    done = None
     for i in range(16):
         qm, om, score, dp = following
         if i < 15:
             following = head_scores(i + 1)
-        if i % 4 == 0:
-            lanes = slice(32 * i, 32 * i + 128)
-            kt = win_k[:, lanes].astype(F32).T.astype(BF)
-            gk = jnp.zeros((256, 128), F32)
-            gv = jnp.zeros((256, 128), F32)
-            gq = []
-        score = score * SCALE + bias[...]
-        e = jnp.exp(score - jnp.max(score, axis=0, keepdims=True))
+        if done is not None:
+            head_grads(i - 1, *done)
+        score = score * (SCALE * LOG2E) + bias[...]
+        e = jnp.exp2(score - jnp.max(score, axis=0, keepdims=True))
         prob = e * (1.0 / jnp.sum(e, axis=0, keepdims=True))
         dp = dp - jnp.sum(prob * dp, axis=0, keepdims=True)
-        ds = (prob * dp * SCALE).astype(BF)
-        gv = gv + nn(prob.astype(BF), om)
-        gk = gk + nn(ds, qm)
-        gq.append(nn(kt[32 * (i % 4):32 * (i % 4) + 32], ds))
-        if i % 4 == 3:
-            g_k[:, lanes] = gk.astype(BF)
-            g_v[:, lanes] = gv.astype(BF)
-            g_q[:, lanes] = jnp.concatenate(gq, axis=0).T.astype(BF)
+        done = (prob.astype(BF), (prob * dp * SCALE).astype(BF), qm, om)
+    head_grads(15, *done)
 
     def shift_grad(at):
         d = nt(g_q[at], full[WQ]) + nt(g_k[at], full[WK]) + nt(g_v[at], full[WV])

time: 51.7 us -> 49.6 us (0.959)
  Pallas kernels: 50.6 us -> 48.5 us
    pallas_call x1, Pallas kernels: 50.6 us -> 48.5 us  [per_device(): pl.pallas_call(kernel, out_shape=pltpu.VMEM((LEVELS, 288, 128), BF), in_s...]
where the time goes in v4:
time: 49.6 us; the launch traced here: 49.5 us
  Pallas kernels  48.5 us (98%)
  local copies, waits for them, and re-layouts  0.94 us (2%)
    pallas_call x1, Pallas kernels, per_device(): pl.pallas_call(kernel, out_shape=pltpu.VMEM((LEVELS, 288, 128), BF), in_s...  48.5 us

profile of v4, /device:TPU:1, one launch (start us, length us, event | category | flops | bytes accessed | tf_op | source)
XLA Modules:
  0.0 49.5 jit_solution(2876415375424929948)
XLA Ops:
  0.0 48.5 %encoder_backward.1 = bf16[13,288,128]{2,1,0:T(8,128)(2,1)S(1)} custom-call(bf16[13,6,48,512]{3,2,1,0:T(8,128)(2,1)} %levels.1, bf16[3,512]{1,0:T(4,128)(2,1)} %lq_in.1, bf16[512,128]{1,0:T(8,128)(2,1)} %wpq_in.1, bf16[512,128]{1,0:T(8,128)(2,1)} %wpk.1, bf16[512,128]{1,0:T(8,128)(2,1)} %wpv.1, bf16[128,512]{1,0:T(8,128)(2,1)} %wpo.1, f32[1,512]{1,0:T(1,128)} %bitcast.3, ...), custom_call_target="tpu_custom_call" | custom-call | tf_op jit(solution)/shard_map/encoder_backward/pallas_call | solution.py:455
  48.5 0.9 %copy.14 = bf16[13,6,48,128]{3,2,1,0:T(8,128)(2,1)} copy(bf16[13,6,48,128]{3,2,1,0:T(8,128)(2,1)S(1)} %bitcast.2) | data formatting | bytes 1916928

commit v5 on v4

--- a/solution.py
+++ b/solution.py
@@ -249,9 +249,9 @@
     relay(PV)
     score_levels(0)
     have(PV)
+    relay(PO)
     project_values(1)
     mixed = mix(1)
-    relay(PO)
     have(PO)
     lat_l[...] = latent_of(mixed)
     send(remote(lat_l, lat_in, e_send.at[1], e_recv.at[1], (after, h)))
@@ -334,7 +334,8 @@
             d - jnp.mean(d, axis=-1, keepdims=True) - z * jnp.mean(d * z, axis=-1, keepdims=True)
         )
 
-    ds_l[...] = shift_grad(slice(128, 256)).astype(BF)
+    shift = shift_grad(slice(0, 256))
+    ds_l[...] = shift[128:].astype(BF)
     send(remote(ds_l, ds_in, e_send.at[2], e_recv.at[2], (prev, h)))
 
     low_lanes = cols(128) < 64
@@ -385,7 +386,7 @@
                 ))
             own_part(half, c).start()
 
-    grad = cot_win[0:128].astype(F32) + shift_grad(slice(0, 128))
+    grad = cot_win[0:128].astype(F32) + shift[:128]
     backward(0, grad.astype(BF))
     remote(ds_l, ds_in, e_send.at[2], e_recv.at[2], (prev, h)).wait_recv()
     grad = cot_l[...].astype(F32) + ds_in[...].astype(F32)

time: 49.6 us -> 49 us (0.988)
  Pallas kernels: 48.5 us -> 47.9 us
    pallas_call x1, Pallas kernels: 48.5 us -> 47.9 us  [per_device(): pl.pallas_call(kernel, out_shape=pltpu.VMEM((LEVELS, 288, 128), BF), in_s...]
where the time goes in v5:
time: 49 us; the launch traced here: 48.9 us
  Pallas kernels  47.9 us (98%)
  local copies, waits for them, and re-layouts  0.94 us (2%)
    pallas_call x1, Pallas kernels, per_device(): pl.pallas_call(kernel, out_shape=pltpu.VMEM((LEVELS, 288, 128), BF), in_s...  47.9 us

profile of v5, /device:TPU:1, one launch (start us, length us, event | category | flops | bytes accessed | tf_op | source)
XLA Modules:
  0.0 48.9 jit_solution(912057113274051119)
XLA Ops:
  0.0 47.9 %encoder_backward.1 = bf16[13,288,128]{2,1,0:T(8,128)(2,1)S(1)} custom-call(bf16[13,6,48,512]{3,2,1,0:T(8,128)(2,1)} %levels.1, bf16[3,512]{1,0:T(4,128)(2,1)} %lq_in.1, bf16[512,128]{1,0:T(8,128)(2,1)} %wpq_in.1, bf16[512,128]{1,0:T(8,128)(2,1)} %wpk.1, bf16[512,128]{1,0:T(8,128)(2,1)} %wpv.1, bf16[128,512]{1,0:T(8,128)(2,1)} %wpo.1, f32[1,512]{1,0:T(1,128)} %bitcast.3, ...), custom_call_target="tpu_custom_call" | custom-call | tf_op jit(solution)/shard_map/encoder_backward/pallas_call | solution.py:456
  47.9 0.9 %copy.14 = bf16[13,6,48,128]{3,2,1,0:T(8,128)(2,1)} copy(bf16[13,6,48,128]{3,2,1,0:T(8,128)(2,1)S(1)} %bitcast.2) | data formatting | bytes 1916928

commit v6 on v5

--- a/solution.py
+++ b/solution.py
@@ -104,7 +104,7 @@
     local = [
         pltpu.make_async_copy(src, dst, loc_sem.at[i]) for i, (src, dst) in enumerate(local)
     ]
-    for copy in local[11:] + local[:11]:
+    for copy in local[11:] + local[1:4:2] + local[0:4:2] + local[4:11]:
         copy.start()
 
     local[11].wait()
@@ -166,19 +166,6 @@
     bias[...] = jnp.where(jnp.logical_or(pad_key, crossing), -1e30, 0.0).astype(F32)
     lq_row = nn(hot(lax.div(rows(128), PART) == cols(16)), lq16)
 
-    local[0].wait()
-    local[2].wait()
-    cell = lax.rem(rows(80), PART)
-    spot = lax.div(rows(80), PART) * 96 + lax.div(cell, 12) * 32 + base + lax.rem(cell, 12)
-    take = hot(jnp.where(cell < 36, spot, -1) == cols(192))
-    for c in range(CHUNKS):
-        got = [nn(take, lev[4 * c + i].reshape(192, WIDTH)) for i in range(DEPTH[c])]
-        for half in range(2):
-            part = [one[PART * half:PART * (half + 1)] for one in got]
-            if DEPTH[c] == 1:
-                part.append(jnp.zeros((8, WIDTH), F32))
-            xs[half, START[c]:START[c] + SIZE[c]] = jnp.concatenate(part, axis=0).astype(BF)
-
     local[1].wait()
     local[3].wait()
     cell = lax.rem(rows(128), PART)
@@ -195,6 +182,19 @@
             send(remote(cot_l, cot_win.at[pl.ds(128, 128)], e_send.at[0], e_recv.at[0], (after, h)))
         else:
             cot_win[0:128] = total.astype(BF)
+
+    local[0].wait()
+    local[2].wait()
+    cell = lax.rem(rows(80), PART)
+    spot = lax.div(rows(80), PART) * 96 + lax.div(cell, 12) * 32 + base + lax.rem(cell, 12)
+    take = hot(jnp.where(cell < 36, spot, -1) == cols(192))
+    for c in range(CHUNKS):
+        got = [nn(take, lev[4 * c + i].reshape(192, WIDTH)) for i in range(DEPTH[c])]
+        for half in range(2):
+            part = [one[PART * half:PART * (half + 1)] for one in got]
+            if DEPTH[c] == 1:
+                part.append(jnp.zeros((8, WIDTH), F32))
+            xs[half, START[c]:START[c] + SIZE[c]] = jnp.concatenate(part, axis=0).astype(BF)
 
     for r, peer in enumerate((sib, over, diag)):
         remote(qbuf.at[peer], qbuf.at[peer], q_send.at[r], q_recv.at[r], (s, peer)).wait_recv()

time: 49 us -> 48.4 us (0.988)
  Pallas kernels: 47.9 us -> 47.4 us
    pallas_call x1, Pallas kernels: 47.9 us -> 47.4 us  [per_device(): pl.pallas_call(kernel, out_shape=pltpu.VMEM((LEVELS, 288, 128), BF), in_s...]
where the time goes in v6:
time: 48.4 us; the launch traced here: 48.3 us
  Pallas kernels  47.4 us (98%)
  local copies, waits for them, and re-layouts  0.94 us (2%)
    pallas_call x1, Pallas kernels, per_device(): pl.pallas_call(kernel, out_shape=pltpu.VMEM((LEVELS, 288, 128), BF), in_s...  47.4 us

profile of v6, /device:TPU:1, one launch (start us, length us, event | category | flops | bytes accessed | tf_op | source)
XLA Modules:
  0.0 48.3 jit_solution(1842488512729297931)
XLA Ops:
  0.0 47.4 %encoder_backward.1 = bf16[13,288,128]{2,1,0:T(8,128)(2,1)S(1)} custom-call(bf16[13,6,48,512]{3,2,1,0:T(8,128)(2,1)} %levels.1, bf16[3,512]{1,0:T(4,128)(2,1)} %lq_in.1, bf16[512,128]{1,0:T(8,128)(2,1)} %wpq_in.1, bf16[512,128]{1,0:T(8,128)(2,1)} %wpk.1, bf16[512,128]{1,0:T(8,128)(2,1)} %wpv.1, bf16[128,512]{1,0:T(8,128)(2,1)} %wpo.1, f32[1,512]{1,0:T(1,128)} %bitcast.3, ...), custom_call_target="tpu_custom_call" | custom-call | tf_op jit(solution)/shard_map/encoder_backward/pallas_call | solution.py:456
  47.4 0.9 %copy.14 = bf16[13,6,48,128]{3,2,1,0:T(8,128)(2,1)} copy(bf16[13,6,48,128]{3,2,1,0:T(8,128)(2,1)S(1)} %bitcast.2) | data formatting | bytes 1916928
